TPU v7x, 128 devices: a whole 4x4x4 slice. The times are simulated.
128 devices in a mesh: trip: 8 (over x, core), exc: 16 (over y, z).
Axes of the slice: x: 4, y: 4, z: 4, core: 2. Of those that a mesh axis runs over, the one named last changes fastest.
Arguments:
- pes_grids: float32 [512, 16, 256], P(('trip', 'exc')), may hold values from -6 to 6
- modals: float32 [200, 128], P('trip'), may hold values from -1.8 to 1.8
- energies: float32 [200, 8], P('trip'), may hold values from 0.05 to 0.5
- triple_modes: int32 [512, 3], P(('trip', 'exc')), may hold values from 0 to 199, as said below
- routing: int32 [8, 16, 16], P('trip', None, 'exc'), may hold values from 0 to 3
- block_source: int32 [3072], P(('trip', 'exc')), may hold values from 0 to 15
- live_rows: int32 [3072], P(('trip', 'exc')), may hold values from 1 to 8
- trial_vectors: bfloat16 [3072, 512, 512], P(('trip', 'exc')), may hold values from -6 to 6
- spectator_energy: float32 [3072, 8], P(('trip', 'exc')), may hold values from 0.1 to 1
Outputs:
- sigma_blocks: bfloat16 [3072, 512, 512], P(('trip', 'exc'))
Inputs may be any that keep to these rules, and one draw needn't show every extreme that they name: `triple_modes`: the three modes of a triple are distinct.
All inputs are finite; a program needn't handle non-finite values.
Results may differ from a plain program's by a relative error of at most 0.005.
Values may be sent and summed in bfloat16 or wider, within the bound.
No kernel may reach another device: no remote copies, remote signals or barrier semaphores. Data moves between devices by JAX's collectives and lax.ppermute only.
A program may use at most 128 MiB of HBM per device.

v0:
```python
import jax
import jax.numpy as jnp
from jax import lax
from jax.experimental import pallas as pl
from jax.experimental.pallas import tpu as pltpu
from jax.sharding import PartitionSpec as P

NMOD = 8
G = 16
NVEC = 64
S = 512
HALF = 256
COLS = 16
TRIPS = 8
TABLE_ROWS = 40
MODAL_ROWS = 32
PAY_ROWS = 32
XOR_STEPS = (1, 2, 6)
F32 = jnp.float32
BF16 = jnp.bfloat16


def iota(shape, axis):
    return lax.broadcasted_iota(jnp.int32, shape, axis)


def pack_kernel(routing, triple_modes, pes, modals, energies, pay, table):
    lane = iota((8, HALF), 1)
    per = modals.shape[0]
    for q in range(COLS):
        local = routing[q]
        pay[q, 0:G, :] = pes[local]
        names = jnp.zeros((8, HALF), F32)
        for n in range(3):
            mode = triple_modes[local, n]
            owner = lax.div(mode, per)
            names = jnp.where(lane == n, owner.astype(F32), names)
            names = jnp.where(lane == 3 + n, (mode - owner * per).astype(F32), names)
        pay[q, G : G + 8, :] = names
    table[...] = jnp.zeros_like(table)
    table[0:per, :] = modals[...]
    table[MODAL_ROWS:TABLE_ROWS, 0:per] = energies[...]


def split(x):
    high = x.astype(BF16)
    return high, (x - high.astype(F32)).astype(BF16)


def pick(values, chosen):
    high, low = split(values)
    return jnp.dot(high, chosen, preferred_element_type=F32) + jnp.dot(
        low, chosen, preferred_element_type=F32
    )


def ones_where(condition):
    return jnp.where(condition, 1.0, 0.0).astype(BF16)


def repeat_rows(x, count):
    rows, lanes = x.shape
    return jnp.broadcast_to(x[:, None, :], (rows, count, lanes)).reshape(rows * count, lanes)


def sigma_kernel(
    sources_live, pay, table, spectator, vectors, out,
    held, matrix, zeros, modal_i, modal_j, modal_k, modal_f, level, spread, used, in_sem, out_sem,
):
    blocks = held.shape[0]
    left, right = pl.ds(0, HALF), pl.ds(HALF, HALF)
    sources, live = sources_live.at[0], sources_live.at[1]

    def load(b, half, n):
        return pltpu.make_async_copy(vectors.at[b, :, half], held.at[b, :, half], in_sem.at[b, n])

    def store(b, half, n):
        return pltpu.make_async_copy(held.at[b, :, half], out.at[b, :, half], out_sem.at[b, n])

    def blank(b):
        return pltpu.make_async_copy(zeros, out.at[b, :, right], out_sem.at[b, 1])

    zeros[...] = jnp.zeros_like(zeros)
    for s in range(COLS):
        used[s] = 0

    @pl.loop(0, blocks)
    def _(b):
        used[sources[b]] = 1
        load(b, left, 0).start()

        @pl.when(live[b] > 4)
        def _():
            load(b, right, 1).start()

    @pl.loop(0, blocks)
    def _(b):
        @pl.when(live[b] <= 4)
        def _():
            blank(b).start()

    me = lax.axis_index("trip")


    def owner_of(slot):
        return (me ^ (slot & 3) ^ jnp.where((slot & 4) > 0, 6, 0)).astype(F32)

    owner = owner_of(iota((1, HALF), 1) // MODAL_ROWS)
    within = (iota((1, HALF), 1) % MODAL_ROWS).astype(F32)
    named = pay[:, G, :]
    owners = [named[:, n : n + 1] for n in range(3)]
    places = [named[:, n + 3 : n + 4] for n in range(3)]
    chosen = jnp.concatenate(
        [ones_where((owners[n] == owner) & (places[n] == within)) for n in range(3)], axis=0
    )
    starts = range(0, table.shape[0], TABLE_ROWS)
    modals = jnp.concatenate([table[n : n + MODAL_ROWS, :] for n in starts], axis=0)
    levels = jnp.concatenate([table[n + MODAL_ROWS : n + TABLE_ROWS, :] for n in starts], axis=0)
    levels = jnp.concatenate([levels, jnp.zeros_like(levels)], axis=0)
    high, low = split(modals)
    rows = jnp.dot(chosen, high, preferred_element_type=F32) + jnp.dot(
        chosen, low, preferred_element_type=F32
    )
    own_modal = iota((128, 128), 1) // G == iota((128, 128), 0) % NMOD
    first, second, third = (
        jnp.where(own_modal, repeat_rows(rows[16 * n : 16 * n + 16], NMOD), 0.0)
        for n in range(3)
    )
    by_major = ones_where(iota((128, HALF), 1) // G == iota((128, HALF), 0) % G)
    by_minor = ones_where(iota((128, HALF), 1) % G == iota((128, HALF), 0) % G)
    modal_i[...] = pick(first, by_major)
    modal_j[...] = pick(second, by_major)
    modal_k[...] = pick(third, by_minor)
    own_point = iota((HALF, 128), 1) % G == iota((HALF, 128), 0) % G
    points = jnp.where(own_point, repeat_rows(rows[0:16], G), 0.0)
    modal_f[...] = pick(points, ones_where(iota((128, S), 0) // G == iota((128, S), 1) // NVEC))
    row, col = iota((128, S), 0), iota((128, S), 1)
    level_high, level_low = split(levels)
    lane = iota((1, 128), 1)
    level_owner = jnp.where(lane < 64, owner_of(lane // NMOD), -1.0)
    total = jnp.zeros((COLS, S), F32)
    for n, digit in enumerate((col // 64, (col // 8) % 8, col % 8)):
        at = ones_where(places[n] == lane.astype(F32))
        found = lax.dot_general(
            at, level_high, (((1,), (1,)), ((), ())), preferred_element_type=F32
        ) + lax.dot_general(at, level_low, (((1,), (1,)), ((), ())), preferred_element_type=F32)
        own = jnp.where(owners[n] == level_owner, found, 0.0)
        total = total + pick(own, ones_where(row % NMOD == digit))
    level[...] = total
    padded = jnp.concatenate([spectator[...], jnp.zeros((blocks, 120), F32)], axis=1)
    spread[...] = pick(padded, ones_where(row == col // NVEC))

    same = iota((128, HALF), 0) % G == iota((128, HALF), 1) % G

    @pl.loop(0, COLS)
    def _(s):
        @pl.when(used[s] > 0)
        def _():
            eight = pl.ds(pl.multiple_of(s * 8, 8), 8)
            sixteen = pl.ds(pl.multiple_of(s * 16, 16), 16)
            grid = pay[s, 0:G, :]
            pairs = (modal_j[eight, :][:, None, :] * modal_k[eight, :][None, :, :]).reshape(64, HALF)
            high, low = split(pairs)
            weights = jnp.concatenate([high, high, low, low], axis=0)
            mix = jnp.where(same, repeat_rows(modal_i[eight, :], G), 0.0).astype(BF16)
            factor = modal_f[sixteen, :]
            levels = level[pl.ds(s, 1), :]
            for r in range(4):
                part = pairs[16 * r : 16 * r + 16]
                scaled = (grid[:, None, :] * part[None, :, :]).reshape(HALF, HALF).astype(BF16)
                both = lax.dot_general(
                    scaled, weights, (((1,), (1,)), ((), ())), preferred_element_type=F32
                )
                inner = (both[:, 0:128] + both[:, 128:256]).reshape(G, G, 128)
                wide = jnp.concatenate(
                    [
                        (inner * factor[:, None, 128 * j : 128 * j + 128])
                        .reshape(HALF, 128)
                        .astype(BF16)
                        for j in range(4)
                    ],
                    axis=1,
                )
                block = jnp.dot(mix, wide, preferred_element_type=F32)
                for a in range(NMOD):
                    tile = slice(128 * (a // 2), 128 * (a // 2) + 128)
                    at = iota((G, 128), 1) == iota((G, 128), 0) + (64 * (a % 2) + 16 * r)
                    mine = block[16 * a : 16 * a + 16, :]
                    target = slice(64 * a + 16 * r, 64 * a + 16 * r + 16)
                    matrix[s, target, :] = mine.astype(BF16)
                    matrix[s, target, tile] = (
                        mine[:, tile] + jnp.where(at, levels[:, tile], 0.0)
                    ).astype(BF16)

    def apply(b, lanes):
        coeff = held[b, :, 0:lanes]
        product = jnp.dot(matrix[sources[b]], coeff, preferred_element_type=F32)
        summed = product + spread[pl.ds(b, 1), 0:lanes] * coeff.astype(F32)
        kept = iota((1, lanes), 1) < live[b] * NVEC
        held[b, :, 0:lanes] = jnp.where(kept, summed, 0.0).astype(BF16)

    @pl.loop(0, blocks)
    def _(b):
        load(b, left, 0).wait()

        @pl.when(live[b] > 4)
        def _():
            load(b, right, 1).wait()
            apply(b, S)
            store(b, right, 1).start()

        @pl.when(live[b] <= 4)
        def _():
            apply(b, HALF)

        store(b, left, 0).start()

    @pl.loop(0, blocks)
    def _(b):
        store(b, left, 0).wait()
        store(b, right, 1).wait()


def late_call(sources, live, received, table, spectator, vectors):
    vmem, smem = pl.BlockSpec(memory_space=pltpu.VMEM), pl.BlockSpec(memory_space=pltpu.SMEM)
    anywhere = pl.BlockSpec(memory_space=pl.ANY)
    blocks = vectors.shape[0]
    return pl.pallas_call(
        sigma_kernel,
        out_shape=jax.ShapeDtypeStruct(vectors.shape, BF16),
        in_specs=[smem, vmem, vmem, vmem, anywhere],
        out_specs=anywhere,
        scratch_shapes=[
            pltpu.VMEM((blocks, S, S), BF16),
            pltpu.VMEM((COLS, S, S), BF16),
            pltpu.VMEM((S, HALF), BF16),
            pltpu.VMEM((128, HALF), F32),
            pltpu.VMEM((128, HALF), F32),
            pltpu.VMEM((128, HALF), F32),
            pltpu.VMEM((HALF, S), F32),
            pltpu.VMEM((COLS, S), F32),
            pltpu.VMEM((blocks, S), F32),
            pltpu.SMEM((COLS,), jnp.int32),
            pltpu.SemaphoreType.DMA((blocks, 2)),
            pltpu.SemaphoreType.DMA((blocks, 2)),
        ],
        compiler_params=pltpu.CompilerParams(vmem_limit_bytes=48 * 2**20),
        cost_estimate=pl.CostEstimate(
            flops=2 * (blocks + COLS) * S**3, bytes_accessed=4 * blocks * S * S, transcendentals=0
        ),
    )(jnp.stack([sources, live]), received, table, spectator, vectors)


def on_device(
    pes_grids,
    modals,
    energies,
    triple_modes,
    routing,
    block_source,
    live_rows,
    trial_vectors,
    spectator_energy,
):
    vmem, smem = pl.BlockSpec(memory_space=pltpu.VMEM), pl.BlockSpec(memory_space=pltpu.SMEM)
    pay, table = pl.pallas_call(
        pack_kernel,
        out_shape=(
            jax.ShapeDtypeStruct((COLS, PAY_ROWS, HALF), F32),
            jax.ShapeDtypeStruct((TABLE_ROWS, 128), F32),
        ),
        in_specs=[smem, smem, vmem, vmem, vmem],
        out_specs=(vmem, vmem),
    )(routing.reshape(COLS), triple_modes, pes_grids, modals, energies.T)
    received = lax.all_to_all(pay, "exc", split_axis=0, concat_axis=0, tiled=True)
    for step in XOR_STEPS:
        other = lax.ppermute(table, "trip", [(n, n ^ step) for n in range(TRIPS)])
        table = jnp.concatenate([table, other], axis=0)

    return late_call(
        block_source, live_rows, received, table, spectator_energy, trial_vectors
    )


def solution(mesh):
    in_specs = (
        P(("trip", "exc"), None, None),
        P("trip", None),
        P("trip", None),
        P(("trip", "exc"), None),
        P("trip", None, "exc"),
        P(("trip", "exc")),
        P(("trip", "exc")),
        P(("trip", "exc"), None, None),
        P(("trip", "exc"), None),
    )
    out_specs = P(("trip", "exc"), None, None)
    return jax.shard_map(
        on_device, mesh=mesh, in_specs=in_specs, out_specs=out_specs, check_vma=False
    )
```

profile of v0, /device:TPU:8, one launch (start us, length us, event | category | flops | bytes accessed | tf_op | source)
XLA Modules:
  0.0 43.3 jit_solution(10029244612278216270)
XLA Ops:
  0.0 1.8 %shard_map.91 = (f32[16,32,256]{2,1,0:T(8,128)}, f32[40,128]{1,0:T(8,128)}) custom-call(s32[16]{0:T(128)} %bitcast.5, s32[4,3]{1,0:T(4,128)} %triple_modes.1, f32[4,16,256]{2,1,0:T(8,128)} %pes.1, f32[25,128]{1,0:T(8,128)} %modals.1, f32[8,25]{1,0:T(8,128)} %bitcast.4), custom_call_target="tpu_custom_call" | custom-call | tf_op jit(solution)/shard_map/pallas_call | solution.py:266
  1.8 0.0 collective-permute-start
  1.9 8.4 %all-to-all-start = ((f32[16,32,256]{2,1,0:T(8,128)}), f32[16,32,256]{2,1,0:T(8,128)S(1)}, u32[]{:S(2)}, u32[]{:S(2)}) async-start(f32[16,32,256]{2,1,0:T(8,128)} %get-tuple-element.7), calls=%async_computation | async-start | bytes 1048576 | tf_op jit(solution)/shard_map/all_to_all | solution.py:275
  10.3 0.0 collective-permute-done
  10.3 0.7 %pad_maximum_fusion.2 = f32[80,128]{1,0:T(8,128)S(1)} fusion(f32[40,128]{1,0:T(8,128)S(1)} %collective-permute-done, f32[40,128]{1,0:T(8,128)} %get-tuple-element.8), kind=kLoop, calls=%fused_computation.2 | loop fusion | flops 10240 | bytes 81920 | tf_op jit(solution)/shard_map/concatenate | solution.py:278
  11.0 1.5 %collective-permute-start.1 = (f32[80,128]{1,0:T(8,128)S(1)}, f32[80,128]{1,0:T(8,128)S(1)}, u32[]{:S(2)}, u32[]{:S(2)}) collective-permute-start(f32[80,128]{1,0:T(8,128)S(1)} %pad_maximum_fusion.2), channel_id=1, source_target_pairs={{0,32},{16,48},{32,0},{48,16},{64,96},{80,112},{96,64},{112,80},{1... | collective-permute-start | bytes 122888 | tf_op jit(solution)/shard_map/ppermute | solution.py:277
  12.5 0.8 %copy.10.spectator = f32[24,8]{1,0:T(8,128)S(1)} copy(f32[24,8]{0,1:T(8,128)} %param.17) | data formatting | bytes 1536 | tf_op args[8]
  13.3 1.8 %collective-permute-done.1 = f32[80,128]{1,0:T(8,128)S(1)} collective-permute-done((f32[80,128]{1,0:T(8,128)S(1)}, f32[80,128]{1,0:T(8,128)S(1)}, u32[]{:S(2)}, u32[]{:S(2)}) %collective-permute-start.1) | collective-permute-done | bytes 40992 | tf_op jit(solution)/shard_map/ppermute | solution.py:277
  15.0 0.7 %pad_maximum_fusion.1 = f32[160,128]{1,0:T(8,128)S(1)} fusion(f32[80,128]{1,0:T(8,128)S(1)} %collective-permute-done.1, f32[40,128]{1,0:T(8,128)S(1)} %collective-permute-done, f32[40,128]{1,0:T(8,128)} %get-tuple-element.8), kind=kLoop, calls=%fused_computation.1 | loop fusion | flops 40960 | bytes 163840 | tf_op jit(solution)/shard_map/concatenate | solution.py:278
  15.7 2.8 %collective-permute-start.2 = (f32[160,128]{1,0:T(8,128)S(1)}, f32[160,128]{1,0:T(8,128)S(1)}, u32[]{:S(2)}, u32[]{:S(2)}) collective-permute-start(f32[160,128]{1,0:T(8,128)S(1)} %pad_maximum_fusion.1), channel_id=1, source_target_pairs={{0,96},{16,112},{32,64},{48,80},{64,32},{80,48},{96,0},{112,16},{1... | collective-permute-start | bytes 245768 | tf_op jit(solution)/shard_map/ppermute | solution.py:277
  18.5 0.7 %pad_add_fusion.sources_live = s32[2,24]{1,0:T(2,128)S(1)} fusion(s32[1,24]{1,0:T(1,128)} %bitcast.6, s32[1,24]{1,0:T(1,128)} %bitcast.7), kind=kLoop, calls=%fused_computation.3 | loop fusion | flops 48 | bytes 384 | tf_op jit(solution)/shard_map/stack | solution.py:251
  19.2 2.2 %collective-permute-done.2 = f32[160,128]{1,0:T(8,128)S(1)} collective-permute-done((f32[160,128]{1,0:T(8,128)S(1)}, f32[160,128]{1,0:T(8,128)S(1)}, u32[]{:S(2)}, u32[]{:S(2)}) %collective-permute-start.2) | collective-permute-done | bytes 81952 | tf_op jit(solution)/shard_map/ppermute | solution.py:277
  21.4 0.7 %pad_maximum_fusion.table = f32[320,128]{1,0:T(8,128)S(1)} fusion(f32[160,128]{1,0:T(8,128)S(1)} %collective-permute-done.2, f32[80,128]{1,0:T(8,128)S(1)} %collective-permute-done.1, f32[40,128]{1,0:T(8,128)S(1)} %collective-permute-done, f32[40,128]{1,0:T(8,128)} %get-tuple-element.8), kind=kLoop, calls=%fused_computation | loop fusion | flops 122880 | bytes 327680 | tf_op jit(solution)/shard_map/concatenate | solution.py:278
  22.1 0.0 all-to-all-done.pay
  22.1 21.1 %shard_map.92 = bf16[24,512,512]{2,1,0:T(8,128)(2,1)} custom-call(s32[2,24]{1,0:T(2,128)S(1)} %pad_add_fusion.sources_live, f32[16,32,256]{2,1,0:T(8,128)S(1)} %all-to-all-done.pay, f32[320,128]{1,0:T(8,128)S(1)} %pad_maximum_fusion.table, f32[24,8]{1,0:T(8,128)S(1)} %copy.10.spectator, bf16[24,512,512]{2,1,0:T(8,128)(2,1)} %vectors.1), custom_call_target="tpu_custom_call" | custom-call | flops 10737418240 | bytes 25165824 | tf_op jit(solution)/shard_map/pallas_call | solution.py:228
Async XLA Ops:
  1.8 8.4 %collective-permute-start = (f32[40,128]{1,0:T(8,128)}, f32[40,128]{1,0:T(8,128)S(1)}, u32[]{:S(2)}, u32[]{:S(2)}) collective-permute-start(f32[40,128]{1,0:T(8,128)} %get-tuple-element.8), channel_id=1, source_target_pairs={{0,16},{16,0},{32,48},{48,32},{64,80},{80,64},{96,112},{112,96},{1... | collective-permute-start | bytes 61448 | tf_op jit(solution)/shard_map/ppermute | solution.py:277
  1.9 20.3 %all-to-all-start = ((f32[16,32,256]{2,1,0:T(8,128)}), f32[16,32,256]{2,1,0:T(8,128)S(1)}, u32[]{:S(2)}, u32[]{:S(2)}) async-start(f32[16,32,256]{2,1,0:T(8,128)} %get-tuple-element.7), calls=%async_computation | async-start | bytes 1048576 | tf_op jit(solution)/shard_map/all_to_all | solution.py:275
  11.0 4.0 %collective-permute-start.1 = (f32[80,128]{1,0:T(8,128)S(1)}, f32[80,128]{1,0:T(8,128)S(1)}, u32[]{:S(2)}, u32[]{:S(2)}) collective-permute-start(f32[80,128]{1,0:T(8,128)S(1)} %pad_maximum_fusion.2), channel_id=1, source_target_pairs={{0,32},{16,48},{32,0},{48,16},{64,96},{80,112},{96,64},{112,80},{1... | collective-permute-start | bytes 122888 | tf_op jit(solution)/shard_map/ppermute | solution.py:277
  15.7 5.7 %collective-permute-start.2 = (f32[160,128]{1,0:T(8,128)S(1)}, f32[160,128]{1,0:T(8,128)S(1)}, u32[]{:S(2)}, u32[]{:S(2)}) collective-permute-start(f32[160,128]{1,0:T(8,128)S(1)} %pad_maximum_fusion.1), channel_id=1, source_target_pairs={{0,96},{16,112},{32,64},{48,80},{64,32},{80,48},{96,0},{112,16},{1... | collective-permute-start | bytes 245768 | tf_op jit(solution)/shard_map/ppermute | solution.py:277
where the time goes:
time: 43.7 us; the launch traced here: 43.3 us
  Pallas kernels  23 us (53%)
  starting transfers between devices  12.7 us (29%)
  waiting for transfers between devices  3.97 us (9%)
  other arithmetic  2.88 us (7%)
  local copies, waits for them, and re-layouts  0.76 us (2%)
    pallas_call x1, Pallas kernels, late_call(): pl.pallas_call(sigma_kernel, out_shape=jax.ShapeDtypeStruct(vectors.shape...  21.1 us
    all_to_all x1, starting transfers between devices, on_device(): lax.all_to_all(pay, 'exc', split_axis=0, concat_axis=0, tiled=True)  8.41 us
    ppermute x3, starting transfers between devices, on_device(): other = lax.ppermute(table, 'trip', [(n, n ^ step) for n in range(TRIPS)])  4.25 us
    ppermute x3, waiting for transfers between devices, on_device(): other = lax.ppermute(table, 'trip', [(n, n ^ step) for n in range(TRIPS)])  3.97 us
    concatenate x3, other arithmetic, on_device(): table = jnp.concatenate([table, other], axis=0)  2.21 us
    pallas_call x1, Pallas kernels, on_device(): pl.pallas_call(pack_kernel, out_shape=(jax.ShapeDtypeStruct((COLS, PAY_RO...  1.85 us
  transfers between devices with their start and end apart: 4, of which 2 were waited for; matrix products, arithmetic and copies ran while one was open for 8% of the time, Pallas kernels for 0%

commit v1 on v0

v1 whole, which is shorter than its diff:
```python
import jax
import jax.numpy as jnp
from jax import lax
from jax.experimental import pallas as pl
from jax.experimental.pallas import tpu as pltpu
from jax.sharding import PartitionSpec as P

NMOD = 8
G = 16
NVEC = 64
S = 512
HALF = 256
COLS = 16
TRIPS = 8
TABLE_ROWS = 40
MODAL_ROWS = 32
PAY_ROWS = 24
UNROLL = 8
F32 = jnp.float32
BF16 = jnp.bfloat16


def iota(shape, axis):
    return lax.broadcasted_iota(jnp.int32, shape, axis)


def pack_kernel(routing, triple_modes, pes, modals, energies, pay, table):
    lane = iota((8, HALF), 1)
    per = modals.shape[0]
    for q in range(COLS):
        local = routing[q]
        pay[q, 0:G, :] = pes[local]
        names = jnp.zeros((8, HALF), F32)
        for n in range(3):
            mode = triple_modes[local, n]
            owner = lax.div(mode, per)
            names = jnp.where(lane == n, owner.astype(F32), names)
            names = jnp.where(lane == 3 + n, (mode - owner * per).astype(F32), names)
        pay[q, G : G + 8, :] = names
    table[...] = jnp.zeros_like(table)
    table[0:per, :] = modals[...]
    table[MODAL_ROWS:TABLE_ROWS, 0:per] = energies[...]


def split(x):
    high = x.astype(BF16)
    return high, (x - high.astype(F32)).astype(BF16)


def pick(values, chosen):
    high, low = split(values)
    return jnp.dot(high, chosen, preferred_element_type=F32) + jnp.dot(
        low, chosen, preferred_element_type=F32
    )


def ones_where(condition):
    return jnp.where(condition, 1.0, 0.0).astype(BF16)


def repeat_rows(x, count):
    rows, lanes = x.shape
    return jnp.broadcast_to(x[:, None, :], (rows, count, lanes)).reshape(rows * count, lanes)


def sigma_kernel(
    sources_live, pay, table_0, table_1, table_2, table_3, spectator, vectors, out,
    held, matrix, folded, summed, modal_j, modal_k, level, spread, used, in_sem, out_sem,
):
    blocks = held.shape[0]
    sources, live = sources_live.at[0], sources_live.at[1]

    def load(b, n):
        at = pl.ds(n * HALF, HALF)
        return pltpu.make_async_copy(vectors.at[b, :, at], held.at[b, :, at], in_sem.at[b, n])

    def store(b):
        return pltpu.make_async_copy(held.at[b], out.at[b], out_sem)

    for s in range(COLS):
        used[s] = 0

    @pl.loop(0, blocks)
    def _(b):
        used[sources[b]] = 1
        load(b, 0).start()

        @pl.when(live[b] > 4)
        def _():
            load(b, 1).start()

    me = lax.axis_index("trip")


    def owner_of(slot):
        return (me ^ (slot & 3) ^ jnp.where((slot & 4) > 0, 6, 0)).astype(F32)

    owner = owner_of(iota((1, HALF), 1) // MODAL_ROWS)
    within = (iota((1, HALF), 1) % MODAL_ROWS).astype(F32)
    named = pay[:, G, :]
    owners = [named[:, n : n + 1] for n in range(3)]
    places = [named[:, n + 3 : n + 4] for n in range(3)]
    chosen = jnp.concatenate(
        [ones_where((owners[n] == owner) & (places[n] == within)) for n in range(3)], axis=0
    )
    tables = [
        table[n : n + TABLE_ROWS, :]
        for table in (table_0, table_1, table_2, table_3)
        for n in (0, TABLE_ROWS)
    ]
    modals = jnp.concatenate([table[0:MODAL_ROWS] for table in tables], axis=0)
    levels = jnp.concatenate([table[MODAL_ROWS:] for table in tables], axis=0)
    levels = jnp.concatenate([levels, jnp.zeros_like(levels)], axis=0)
    high, low = split(modals)
    rows = jnp.dot(chosen, high, preferred_element_type=F32) + jnp.dot(
        chosen, low, preferred_element_type=F32
    )
    own_modal = iota((128, 128), 1) // G == iota((128, 128), 0) % NMOD
    first, second, third = (
        jnp.where(own_modal, repeat_rows(rows[16 * n : 16 * n + 16], NMOD), 0.0)
        for n in range(3)
    )
    by_major = ones_where(iota((128, HALF), 1) // G == iota((128, HALF), 0) % G)
    by_minor = ones_where(iota((128, HALF), 1) % G == iota((128, HALF), 0) % G)
    points = jnp.where(
        iota((128, HALF), 1) // G == iota((128, HALF), 0) // NMOD, pick(first, by_minor), 0.0
    ).reshape(COLS, NMOD, 1, HALF)
    squares = (points * points.reshape(COLS, 1, NMOD, HALF)).reshape(COLS * 64, HALF)
    high, low = split(squares)
    grid_high, grid_low = split(pay[:, 0:G, :].reshape(HALF, HALF))
    summed[...] = (
        jnp.dot(high, grid_high, preferred_element_type=F32)
        + jnp.dot(low, grid_high, preferred_element_type=F32)
        + jnp.dot(high, grid_low, preferred_element_type=F32)
    )
    modal_j[...] = pick(second, by_major)
    modal_k[...] = pick(third, by_minor)
    row, col = iota((128, 2 * S), 0), iota((128, 2 * S), 1)
    level_high, level_low = split(levels)
    lane = iota((1, 128), 1)
    level_owner = jnp.where(lane < 64, owner_of(lane // NMOD), -1.0)
    total = jnp.zeros((COLS, 2 * S), F32)
    for n, digit in enumerate((col // 128, (col // 8) % 8, col % 8)):
        at = ones_where(places[n] == lane.astype(F32))
        found = lax.dot_general(
            at, level_high, (((1,), (1,)), ((), ())), preferred_element_type=F32
        ) + lax.dot_general(at, level_low, (((1,), (1,)), ((), ())), preferred_element_type=F32)
        own = jnp.where(owners[n] == level_owner, found, 0.0)
        total = total + pick(own, ones_where(row % NMOD == digit))
    level[...] = total
    padded = jnp.concatenate([spectator[...], jnp.zeros((blocks, 120), F32)], axis=1)
    spread[...] = pick(padded, ones_where(iota((128, S), 0) == iota((128, S), 1) // NVEC))

    on_left = iota((64, 128), 1) < 64
    on_diagonal = iota((64, 128), 1) % 64 == iota((64, 128), 0)

    @pl.loop(0, COLS)
    def _(s):
        @pl.when(used[s] > 0)
        def _():
            eight = pl.ds(pl.multiple_of(s * 8, 8), 8)
            pairs = (modal_j[eight, :][:, None, :] * modal_k[eight, :][None, :, :]).reshape(64, HALF)
            half = pairs.astype(BF16)
            weights = jnp.concatenate([half, half], axis=0)
            levels = level[pl.ds(s, 1), :]
            place = {}
            for a in range(NMOD):
                others = NMOD - a
                grid = summed[pl.ds(pl.multiple_of(s * 64, 64) + a * NMOD, NMOD), :]
                scaled = (grid[a:, None, :] * pairs[None, :, :]).reshape(64 * others, HALF)
                blocks_of = lax.dot_general(
                    scaled.astype(BF16), weights, (((1,), (1,)), ((), ())), preferred_element_type=F32
                )
                for n in range(others):
                    place[a, a + n] = place[a + n, a] = 64 * (len(set(place.values())))
                    one = blocks_of[64 * n : 64 * n + 64, :]
                    if n == 0:
                        one = one + jnp.where(
                            on_diagonal, levels[:, 128 * a : 128 * a + 128], 0.0
                        )
                    at = place[a, a + n]
                    folded[at : at + 64, :] = one.astype(BF16)
            for a in range(NMOD):
                for j in range(NMOD // 2):
                    even, odd = place[a, 2 * j], place[a, 2 * j + 1]
                    matrix[s, j, 64 * a : 64 * a + 64, :] = jnp.where(
                        on_left, folded[even : even + 64, :], folded[odd : odd + 64, :]
                    )

    def product(b):
        whole = jnp.concatenate([matrix[sources[b], n] for n in range(4)], axis=1)
        return jnp.dot(whole, held[b], preferred_element_type=F32)

    def finish(b, block):
        scale = spread[pl.ds(b, 1), :]
        kept = iota((1, S), 1) < live[b] * NVEC
        summed_up = block + scale * held[b].astype(F32)
        held[b] = jnp.where(kept, summed_up, 0.0).astype(BF16)
        store(b).start()

    @pl.loop(0, blocks // UNROLL)
    def _(step):
        first = step * UNROLL
        for n in range(UNROLL):
            load(first + n, 0).wait()

            @pl.when(live[first + n] > 4)
            def _(n=n):
                load(first + n, 1).wait()

        block = product(first)
        for n in range(UNROLL):
            later = product(first + n + 1) if n + 1 < UNROLL else None
            finish(first + n, block)
            block = later

    pltpu.make_async_copy(held, out, out_sem).wait()


def late_call(sources, live, received, tables, spectator, vectors):
    vmem, smem = pl.BlockSpec(memory_space=pltpu.VMEM), pl.BlockSpec(memory_space=pltpu.SMEM)
    anywhere = pl.BlockSpec(memory_space=pl.ANY)
    blocks = vectors.shape[0]
    return pl.pallas_call(
        sigma_kernel,
        out_shape=jax.ShapeDtypeStruct(vectors.shape, BF16),
        in_specs=[smem, vmem, vmem, vmem, vmem, vmem, vmem, anywhere],
        out_specs=anywhere,
        scratch_shapes=[
            pltpu.VMEM((blocks, S, S), BF16),
            pltpu.VMEM((COLS, 4, S, 128), BF16),
            pltpu.VMEM((36 * 64, 128), BF16),
            pltpu.VMEM((COLS * 64, HALF), F32),
            pltpu.VMEM((128, HALF), F32),
            pltpu.VMEM((128, HALF), F32),
            pltpu.VMEM((COLS, 2 * S), F32),
            pltpu.VMEM((blocks, S), F32),
            pltpu.SMEM((COLS,), jnp.int32),
            pltpu.SemaphoreType.DMA((blocks, 2)),
            pltpu.SemaphoreType.DMA,
        ],
        compiler_params=pltpu.CompilerParams(vmem_limit_bytes=48 * 2**20),
        cost_estimate=pl.CostEstimate(
            flops=2 * (blocks + COLS) * S**3, bytes_accessed=4 * blocks * S * S, transcendentals=0
        ),
    )(jnp.stack([sources, live]), received, *tables, spectator, vectors)


def on_device(
    pes_grids,
    modals,
    energies,
    triple_modes,
    routing,
    block_source,
    live_rows,
    trial_vectors,
    spectator_energy,
):
    vmem, smem = pl.BlockSpec(memory_space=pltpu.VMEM), pl.BlockSpec(memory_space=pltpu.SMEM)
    pay, table = pl.pallas_call(
        pack_kernel,
        out_shape=(
            jax.ShapeDtypeStruct((COLS, PAY_ROWS, HALF), F32),
            jax.ShapeDtypeStruct((TABLE_ROWS, 128), F32),
        ),
        in_specs=[smem, smem, vmem, vmem, vmem],
        out_specs=(vmem, vmem),
    )(routing.reshape(COLS), triple_modes, pes_grids, modals, energies.T)
    received = lax.all_to_all(pay, "exc", split_axis=0, concat_axis=0, tiled=True)

    def swap(x, step):
        return lax.ppermute(x, "trip", [(n, n ^ step) for n in range(TRIPS)])

    both = jnp.concatenate([table, swap(table, 1)], axis=0)
    near, far = swap(both, 2), swap(both, 6)
    tables = (both, near, far, swap(near, 6))
    return late_call(
        block_source, live_rows, received, tables, spectator_energy, trial_vectors
    )


def solution(mesh):
    in_specs = (
        P(("trip", "exc"), None, None),
        P("trip", None),
        P("trip", None),
        P(("trip", "exc"), None),
        P("trip", None, "exc"),
        P(("trip", "exc")),
        P(("trip", "exc")),
        P(("trip", "exc"), None, None),
        P(("trip", "exc"), None),
    )
    out_specs = P(("trip", "exc"), None, None)
    return jax.shard_map(
        on_device, mesh=mesh, in_specs=in_specs, out_specs=out_specs, check_vma=False
    )
```

time: 43.7 us -> 39.7 us (0.908)
  the two profiles are of different devices: /device:TPU:8 before, /device:TPU:40 now
where the time goes in v1:
time: 39.7 us; the launch traced here: 39.8 us
  Pallas kernels  21.3 us (54%)
  starting transfers between devices  14.3 us (36%)
  waiting for transfers between devices  2.09 us (5%)
  local copies, waits for them, and re-layouts  1.49 us (4%)
  other arithmetic  0.68 us (2%)
    pallas_call x1, Pallas kernels, late_call(): pl.pallas_call(sigma_kernel, out_shape=jax.ShapeDtypeStruct(vectors.shape...  19.5 us
    all_to_all x1, starting transfers between devices, on_device(): lax.all_to_all(pay, 'exc', split_axis=0, concat_axis=0, tiled=True)  7.95 us
    ppermute x4, starting transfers between devices, swap(): return lax.ppermute(x, 'trip', [(n, n ^ step) for n in range(TRIPS)])  6.35 us
    ppermute x4, waiting for transfers between devices, swap(): return lax.ppermute(x, 'trip', [(n, n ^ step) for n in range(TRIPS)])  2.09 us
    pallas_call x1, Pallas kernels, on_device(): pl.pallas_call(pack_kernel, out_shape=(jax.ShapeDtypeStruct((COLS, PAY_RO...  1.8 us
    unnamed x2, local copies, waits for them, and re-layouts  1.49 us
  transfers between devices with their start and end apart: 5, of which 3 were waited for; matrix products, arithmetic and copies ran while one was open for 5% of the time, Pallas kernels for 0%

profile of v1, /device:TPU:40, one launch (start us, length us, event | category | flops | bytes accessed | tf_op | source)
XLA Modules:
  0.0 39.8 jit_solution(6702864144005751726)
XLA Ops:
  0.0 1.8 %shard_map.91 = (f32[16,24,256]{2,1,0:T(8,128)}, f32[40,128]{1,0:T(8,128)}) custom-call(s32[16]{0:T(128)} %bitcast.5, s32[4,3]{1,0:T(4,128)} %triple_modes.1, f32[4,16,256]{2,1,0:T(8,128)} %pes.1, f32[25,128]{1,0:T(8,128)} %modals.1, f32[8,25]{1,0:T(8,128)} %bitcast.4), custom_call_target="tpu_custom_call" | custom-call | tf_op jit(solution)/shard_map/pallas_call | solution.py:261
  1.8 8.0 %all-to-all-start = ((f32[16,24,256]{2,1,0:T(8,128)}), f32[16,24,256]{2,1,0:T(8,128)S(1)}, u32[]{:S(2)}, u32[]{:S(2)}) async-start(f32[16,24,256]{2,1,0:T(8,128)} %get-tuple-element.7), calls=%async_computation | async-start | bytes 786432 | tf_op jit(solution)/shard_map/all_to_all | solution.py:270
  9.8 0.0 collective-permute-start
  9.8 0.7 %constant_dynamic-update-slice_fusion.1 = f32[80,128]{1,0:T(8,128)S(1)} fusion(f32[40,128]{1,0:T(8,128)} %get-tuple-element.8), kind=kLoop, calls=%fused_computation.1 | loop fusion | bytes 40960
  10.5 0.7 %collective-permute-done = f32[40,128]{1,0:T(8,128)S(1)} collective-permute-done((f32[40,128]{1,0:T(8,128)}, f32[40,128]{1,0:T(8,128)S(1)}, u32[]{:S(2)}, u32[]{:S(2)}) %collective-permute-start) | collective-permute-done | bytes 20512 | tf_op jit(solution)/shard_map/ppermute | solution.py:273
  11.2 1.5 %collective-permute-start.1 = (f32[80,128]{1,0:T(8,128)S(1)}, f32[80,128]{1,0:T(8,128)S(1)}, u32[]{:S(2)}, u32[]{:S(2)}) collective-permute-start(f32[80,128]{1,0:T(8,128)S(1)} %constant_dynamic-update-slice_fusion.table_0), channel_id=1, source_target_pairs={{0,32},{16,48},{32,0},{48,16},{64,96},{80,112},{96,64},{112,80},{1... | collective-permute-start | bytes 122888 | tf_op jit(solution)/shard_map/ppermute | solution.py:273
  12.7 2.1 %collective-permute-start.2 = (f32[80,128]{1,0:T(8,128)S(1)}, f32[80,128]{1,0:T(8,128)S(1)}, u32[]{:S(2)}, u32[]{:S(2)}) collective-permute-start(f32[80,128]{1,0:T(8,128)S(1)} %constant_dynamic-update-slice_fusion.table_0), channel_id=1, source_target_pairs={{0,96},{16,112},{32,64},{48,80},{64,32},{80,48},{96,0},{112,16},{1... | collective-permute-start | bytes 122888 | tf_op jit(solution)/shard_map/ppermute | solution.py:273
  14.7 0.4 %collective-permute-done.1.table_1 = f32[80,128]{1,0:T(8,128)S(1)} collective-permute-done((f32[80,128]{1,0:T(8,128)S(1)}, f32[80,128]{1,0:T(8,128)S(1)}, u32[]{:S(2)}, u32[]{:S(2)}) %collective-permute-start.1) | collective-permute-done | bytes 40992 | tf_op jit(solution)/shard_map/ppermute | solution.py:273
  15.2 2.8 %collective-permute-start.3 = (f32[80,128]{1,0:T(8,128)S(1)}, f32[80,128]{1,0:T(8,128)S(1)}, u32[]{:S(2)}, u32[]{:S(2)}) collective-permute-start(f32[80,128]{1,0:T(8,128)S(1)} %collective-permute-done.1.table_1), channel_id=1, source_target_pairs={{0,96},{16,112},{32,64},{48,80},{64,32},{80,48},{96,0},{112,16},{1... | collective-permute-start | bytes 122888 | tf_op jit(solution)/shard_map/ppermute | solution.py:273
  17.9 0.7 %pad_add_fusion.sources_live = s32[2,24]{1,0:T(2,128)S(1)} fusion(s32[1,24]{1,0:T(1,128)} %bitcast.6, s32[1,24]{1,0:T(1,128)} %bitcast.7), kind=kLoop, calls=%fused_computation.2 | loop fusion | flops 48 | bytes 384 | tf_op jit(solution)/shard_map/stack | solution.py:246
  18.6 0.8 %copy.10.spectator = f32[24,8]{1,0:T(8,128)S(1)} copy(f32[24,8]{0,1:T(8,128)} %param.17) | data formatting | bytes 1536 | tf_op args[8]
  19.4 0.0 collective-permute-done.2.table_2
  19.4 1.0 %collective-permute-done.3.table_3 = f32[80,128]{1,0:T(8,128)S(1)} collective-permute-done((f32[80,128]{1,0:T(8,128)S(1)}, f32[80,128]{1,0:T(8,128)S(1)}, u32[]{:S(2)}, u32[]{:S(2)}) %collective-permute-start.3) | collective-permute-done | bytes 40992 | tf_op jit(solution)/shard_map/ppermute | solution.py:273
  20.4 0.0 all-to-all-done.pay
  20.4 19.5 %shard_map.92 = bf16[24,512,512]{2,1,0:T(8,128)(2,1)} custom-call(s32[2,24]{1,0:T(2,128)S(1)} %pad_add_fusion.sources_live, f32[16,24,256]{2,1,0:T(8,128)S(1)} %all-to-all-done.pay, f32[80,128]{1,0:T(8,128)S(1)} %constant_dynamic-update-slice_fusion.table_0, f32[80,128]{1,0:T(8,128)S(1)} %collective-permute-done.1.table_1, ...), custom_call_target="tpu_custom_call" | custom-call | flops 10737418240 | bytes 25165824 | tf_op jit(solution)/shard_map/pallas_call | solution.py:224
  (1 shorter events, 0.0 us)
Async XLA Ops:
  1.8 18.6 %all-to-all-start = ((f32[16,24,256]{2,1,0:T(8,128)}), f32[16,24,256]{2,1,0:T(8,128)S(1)}, u32[]{:S(2)}, u32[]{:S(2)}) async-start(f32[16,24,256]{2,1,0:T(8,128)} %get-tuple-element.7), calls=%async_computation | async-start | bytes 786432 | tf_op jit(solution)/shard_map/all_to_all | solution.py:270
  9.8 1.4 %collective-permute-start = (f32[40,128]{1,0:T(8,128)}, f32[40,128]{1,0:T(8,128)S(1)}, u32[]{:S(2)}, u32[]{:S(2)}) collective-permute-start(f32[40,128]{1,0:T(8,128)} %get-tuple-element.8), channel_id=1, source_target_pairs={{0,16},{16,0},{32,48},{48,32},{64,80},{80,64},{96,112},{112,96},{1... | collective-permute-start | bytes 61448 | tf_op jit(solution)/shard_map/ppermute | solution.py:273
  11.2 4.0 %collective-permute-start.1 = (f32[80,128]{1,0:T(8,128)S(1)}, f32[80,128]{1,0:T(8,128)S(1)}, u32[]{:S(2)}, u32[]{:S(2)}) collective-permute-start(f32[80,128]{1,0:T(8,128)S(1)} %constant_dynamic-update-slice_fusion.table_0), channel_id=1, source_target_pairs={{0,32},{16,48},{32,0},{48,16},{64,96},{80,112},{96,64},{112,80},{1... | collective-permute-start | bytes 122888 | tf_op jit(solution)/shard_map/ppermute | solution.py:273
  12.7 6.7 %collective-permute-start.2 = (f32[80,128]{1,0:T(8,128)S(1)}, f32[80,128]{1,0:T(8,128)S(1)}, u32[]{:S(2)}, u32[]{:S(2)}) collective-permute-start(f32[80,128]{1,0:T(8,128)S(1)} %constant_dynamic-update-slice_fusion.table_0), channel_id=1, source_target_pairs={{0,96},{16,112},{32,64},{48,80},{64,32},{80,48},{96,0},{112,16},{1... | collective-permute-start | bytes 122888 | tf_op jit(solution)/shard_map/ppermute | solution.py:273
  15.2 5.2 %collective-permute-start.3 = (f32[80,128]{1,0:T(8,128)S(1)}, f32[80,128]{1,0:T(8,128)S(1)}, u32[]{:S(2)}, u32[]{:S(2)}) collective-permute-start(f32[80,128]{1,0:T(8,128)S(1)} %collective-permute-done.1.table_1), channel_id=1, source_target_pairs={{0,96},{16,112},{32,64},{48,80},{64,32},{80,48},{96,0},{112,16},{1... | collective-permute-start | bytes 122888 | tf_op jit(solution)/shard_map/ppermute | solution.py:273
